TPU v7x, 256 devices: a whole 4x4x8 slice. The times are simulated.
256 devices in a mesh: cache: 32 (over z, x), head: 8 (over y, core).
Axes of the slice: x: 4, y: 4, z: 8, core: 2. Of those that a mesh axis runs over, the one named last changes fastest.
Arguments:
- tokens: bfloat16 [8192, 1024], P('cache', 'head'), may hold values from -6 to 6
- request_user: int32 [32, 1], replicated, may hold values from 0 to 15
- hist_len: int32 [16], replicated, may hold values from 1 to 4096, 40960 in all
- history: bfloat16 [2, 16, 4096, 2048], P(None, None, 'cache', 'head'), may hold values from -6 to 6
- w_in: bfloat16 [2, 1024, 2048], P(None, None, 'head'), may hold values from -0.1875 to 0.1875
- w_out: bfloat16 [2, 1024, 1024], P(None, 'head'), may hold values from -0.1875 to 0.1875
Outputs:
- scored: bfloat16 [8192, 1024], P('cache', 'head')
Inputs may be any that keep to these rules, and one draw needn't show every extreme that they name: `request_user`: every one of the 16 users is named by at least one request.
All inputs are finite; a program needn't handle non-finite values.
Results may differ from a plain program's by a relative error of at most 0.0095.
Values may be sent and summed in bfloat16 or wider, within the bound.
A program may use at most 64 MiB of HBM per device.

v0:
```python
import jax
import jax.numpy as jnp
from jax import lax
from jax.sharding import PartitionSpec as P

H = 16
DH = 64
LAYERS = 2
CAND = 256


def attend_local(queries, key_value, lengths, first_event, local_heads):
    req_count = key_value.shape[0]
    event_count = key_value.shape[1]
    blocks = key_value.reshape(req_count, event_count, local_heads, 2, DH)
    scores = jnp.einsum(
        "rchd,rehd->rhce", queries, blocks[:, :, :, 0, :], preferred_element_type=jnp.float32
    )
    weights = jax.nn.silu(scores * DH ** (-0.5))
    positions = first_event + jnp.arange(event_count, dtype=jnp.int32)
    live_mask = positions[None, :] < lengths[:, None]
    weights = jnp.where(live_mask[:, None, None, :], weights, 0.0).astype(jnp.bfloat16)
    attended = jnp.einsum(
        "rhce,rehd->rchd", weights, blocks[:, :, :, 1, :], preferred_element_type=jnp.float32
    )
    return attended.reshape(req_count * queries.shape[1], local_heads * DH)


def body(tokens, request_user, hist_len, history, w_in, w_out):
    tok_rows = tokens.shape[0]
    head_width = w_out.shape[1]
    local_heads = head_width // DH
    event_count = history.shape[2]
    cache_index = lax.axis_index("cache")
    user_ids = request_user[:, 0]
    matches = user_ids[:, None] == jnp.arange(hist_len.shape[0], dtype=jnp.int32)[None, :]
    user_lengths = jnp.sum(jnp.where(matches, hist_len[None, :], 0), axis=1)
    hidden = tokens
    for layer_index in range(LAYERS):
        w_layer = w_in[layer_index]
        projected = jnp.dot(
            lax.all_gather(hidden, "head", axis=1, tiled=True),
            w_layer,
            preferred_element_type=jnp.float32,
        )
        projected = projected.reshape(tok_rows, local_heads, 2, DH)
        gate_part = jax.nn.silu(projected[:, :, 0, :]).reshape(tok_rows, head_width)
        queries = jax.nn.silu(projected[:, :, 1, :]).astype(jnp.bfloat16)
        layer_hist = history[layer_index]
        all_queries = lax.all_gather(
            queries.reshape(tok_rows, head_width), "cache", axis=0, tiled=True
        )
        part_queries = all_queries
        part_queries = part_queries.reshape(
            tok_rows * lax.axis_size("cache") // CAND, CAND, local_heads, DH
        )
        part_history = jnp.take(layer_hist, user_ids, axis=0)
        attended = lax.psum_scatter(
            attend_local(
                part_queries, part_history, user_lengths, cache_index * event_count, local_heads
            ),
            "cache",
            scatter_dimension=0,
            tiled=True,
        )
        row_sum, row_squares = lax.psum(
            (jnp.sum(attended, axis=1), jnp.sum(attended * attended, axis=1)), "head"
        )
        row_mean = row_sum / (H * DH)
        row_var = row_squares / (H * DH) - row_mean * row_mean
        normed = (
            (attended - row_mean[:, None]) * lax.rsqrt(row_var + 1e-05)[:, None] * gate_part
        ).astype(jnp.bfloat16)
        branch_terms = jnp.dot(normed, w_out[layer_index], preferred_element_type=jnp.float32)
        branch = lax.psum_scatter(branch_terms, "head", scatter_dimension=1, tiled=True)
        hidden = (hidden.astype(jnp.float32) + branch).astype(jnp.bfloat16)
    return hidden


def solution(mesh):
    in_specs = (
        P("cache", "head"),
        P(),
        P(),
        P(None, None, "cache", "head"),
        P(None, None, "head"),
        P(None, "head", None),
    )
    out_specs = P("cache", "head")
    return jax.shard_map(body, mesh=mesh, in_specs=in_specs, out_specs=out_specs, check_vma=False)
```

profile of v0, /device:TPU:1, one launch (start us, length us, event | category | flops | bytes accessed | tf_op | source)
XLA Modules:
  0.0 775.4 jit_solution(1044011529763732283)
XLA Ops:
  6.5 15.5 %all_gather.12 = bf16[256,1024]{1,0:T(8,128)(2,1)S(1)} all-gather(bf16[256,128]{1,0:T(8,128)(2,1)} %param.8), channel_id=1, replica_groups=mesh['cache'=32,'head'=8] {'head'}, dimensions={1}, use_global_device_ids=true | all-gather | bytes 589824 | tf_op jit(solution)/shard_map/all_gather | solution.py:42
  22.1 1.3 slice_bitcast_fusion.13
  23.3 0.2 copy.33
  23.5 0.3 fusion.14
  23.9 0.7 fusion.36
  24.6 0.0 all-gather.3.cloned.1.call-update
  24.6 0.0 reduce-scatter.5.cloned.1.call-start
  24.7 1.7 slice_bitcast_fusion.10
  26.4 2.0 gather_fusion.1
  28.4 2.0 gather_fusion
  30.4 4.0 broadcast_select_fusion
  34.4 4.1 copy.31
  38.5 0.1 select_reduce_fusion
  38.6 0.1 broadcast_compare_fusion
  38.7 58.4 %all-gather.3.cloned.1.call-done = bf16[8192,128]{0,1:T(8,128)(2,1)} async-done(((bf16[256,128]{0,1:T(8,128)(2,1)}), bf16[8192,128]{0,1:T(8,128)(2,1)}) %all-gather.3.cloned.1.call-update) | async-done | bytes 2097168 | tf_op jit(solution)/shard_map/all_gather | solution.py:50
  97.0 3.5 copy.49
  100.5 10.0 %fusion.7 = f32[32,256,2,64]{1,3,2,0:T(8,128)} fusion(pred[32,128]{1,0:T(8,128)(4,1)S(1)} %broadcast_compare_fusion, bf16[32,256,2,64]{1,0,3,2:T(8,128)(2,1)} %bitcast.151, bf16[32,128,2,2,64]{1,4,3,2,0:T(8,128)(2,1)} %bitcast.147), kind=kOutput, calls=%fused_computation.9 | convolution fusion | flops 551550976 | bytes 8392704 | tf_op jit(solution)/shard_map/rhce,rehd->rchd/dot_general | solution.py:23
  110.5 4.6 copy.36
  115.2 5.5 copy.50
  120.7 0.0 reduce-scatter.7.cloned.1.call-start
  120.7 218.5 %reduce-scatter.5.cloned.1.call-done = f32[256,128]{0,1:T(8,128)} async-done(((f32[8192,128]{0,1:T(8,128)}), f32[256,128]{0,1:T(8,128)}) %reduce-scatter.5.cloned.1.call-update) | async-done | bytes 131088 | tf_op jit(solution)/shard_map/reduce_scatter | solution.py:58
  339.2 0.9 fusion.47
  340.2 17.6 %all-reduce.1 = (f32[256]{0:T(256)S(1)}, f32[256]{0:T(256)S(1)}) all-reduce(f32[256]{0:T(256)S(1)} %get-tuple-element.9, f32[256]{0:T(256)S(1)} %get-tuple-element.8), channel_id=1, replica_groups=mesh['cache'=32,'head'=8] {'head'}, use_global_device_ids=true, to_apply=%region_5.7 | all-reduce | flops 512 | bytes 4096 | tf_op jit(solution)/shard_map/psum | solution.py:66
  357.8 1.0 fusion.38
  358.8 2.2 fusion.18
  361.0 0.0 reduce-scatter.7.cloned.1.call-update
  361.0 0.0 all-gather.5.cloned.1.call-start
  361.1 0.2 copy.39
  361.3 27.8 %reduce-scatter.7.cloned.1.call-done = f32[256,128]{1,0:T(8,128)} async-done(((f32[256,1024]{1,0:T(8,128)}), f32[256,128]{1,0:T(8,128)}) %reduce-scatter.7.cloned.1.call-update) | async-done | bytes 131088 | tf_op jit(solution)/shard_map/reduce_scatter | solution.py:75
  389.1 0.9 add_convert_fusion.1
  390.0 15.2 %all_gather.14 = bf16[256,1024]{1,0:T(8,128)(2,1)S(1)} all-gather(bf16[256,128]{1,0:T(8,128)(2,1)S(1)} %add_convert_fusion.1), channel_id=1, replica_groups=mesh['cache'=32,'head'=8] {'head'}, dimensions={1}, use_global_device_ids=true | all-gather | bytes 589824 | tf_op jit(solution)/shard_map/all_gather | solution.py:42
  405.2 0.3 fusion.12
  405.6 0.7 fusion.37
  406.3 0.0 reduce-scatter.9.cloned.1.call-start
  406.3 2.9 copy.37
  409.2 69.5 %all-gather.5.cloned.1.call-done = bf16[8192,128]{0,1:T(8,128)(2,1)} async-done(((bf16[256,128]{0,1:T(8,128)(2,1)}), bf16[8192,128]{0,1:T(8,128)(2,1)}) %all-gather.5.cloned.1.call-update) | async-done | bytes 2097168 | tf_op jit(solution)/shard_map/all_gather | solution.py:50
  478.7 3.7 copy.51
  482.3 7.1 fusion.6
  489.5 4.6 copy.42
  494.1 5.2 copy.52
  499.3 0.0 reduce-scatter.11.cloned.1.call-start
  499.4 218.6 %reduce-scatter.9.cloned.1.call-done = f32[256,128]{0,1:T(8,128)} async-done(((f32[8192,128]{0,1:T(8,128)}), f32[256,128]{0,1:T(8,128)}) %reduce-scatter.9.cloned.1.call-update) | async-done | bytes 131088 | tf_op jit(solution)/shard_map/reduce_scatter | solution.py:58
  718.0 0.9 fusion.46
  718.9 17.7 %all-reduce = (f32[256]{0:T(256)S(1)}, f32[256]{0:T(256)S(1)}) all-reduce(f32[256]{0:T(256)S(1)} %get-tuple-element.7, f32[256]{0:T(256)S(1)} %get-tuple-element.6), channel_id=1, replica_groups=mesh['cache'=32,'head'=8] {'head'}, use_global_device_ids=true, to_apply=%region_11.13 | all-reduce | flops 512 | bytes 4096 | tf_op jit(solution)/shard_map/psum | solution.py:66
  736.6 1.0 fusion.39
  737.6 1.3 fusion.16
  738.9 28.1 %reduce-scatter.11.cloned.1.call-done = f32[256,128]{1,0:T(8,128)} async-done(((f32[256,1024]{1,0:T(8,128)}), f32[256,128]{1,0:T(8,128)}) %reduce-scatter.11.cloned.1.call-update) | async-done | bytes 131088 | tf_op jit(solution)/shard_map/reduce_scatter | solution.py:75
  767.0 1.5 add_convert_fusion
  (23 shorter events, 0.2 us)
Async XLA Ops:
  6.5 90.5 %all-gather.3.cloned.1.call-start = ((), (), s32[]{:S(2)}) async-start(), calls=%async_computation.4 | async-start | bytes 2162688 | tf_op jit(solution)/shard_map/all_gather | solution.py:50
  23.3 1.4 copy-start.4
  24.6 314.6 %reduce-scatter.5.cloned.1.call-start = ((), (), s32[]{:S(2)}) async-start(), calls=%async_computation.5 | async-start | bytes 4325376 | tf_op jit(solution)/shard_map/reduce_scatter | solution.py:58
  34.4 4.1 copy-start.3
  120.6 268.4 %copy-start.2 = (bf16[256,128]{1,0:T(8,128)(2,1)S(1)}, bf16[256,128]{1,0:T(8,128)(2,1)}, u32[]{:S(2)}) copy-start(bf16[256,128]{1,0:T(8,128)(2,1)} %param.8) | copy-start | bytes 196612
  120.7 268.4 %reduce-scatter.7.cloned.1.call-start = ((), (), s32[]{:S(2)}) async-start(), calls=%async_computation.6 | async-start | bytes 1179648 | tf_op jit(solution)/shard_map/reduce_scatter | solution.py:75
  361.0 117.6 %all-gather.5.cloned.1.call-start = ((), (), s32[]{:S(2)}) async-start(), calls=%async_computation.7 | async-start | bytes 2162688 | tf_op jit(solution)/shard_map/all_gather | solution.py:50
  406.3 311.7 %reduce-scatter.9.cloned.1.call-start = ((), (), s32[]{:S(2)}) async-start(), calls=%async_computation.8 | async-start | bytes 4325376 | tf_op jit(solution)/shard_map/reduce_scatter | solution.py:58
  478.7 3.7 copy-start
  499.3 238.2 %copy-start.1 = (bf16[2,128,1024]{2,1,0:T(8,128)(2,1)S(1)}, bf16[2,128,1024]{2,1,0:T(8,128)(2,1)}, u32[]{:S(2)}) copy-start(bf16[2,128,1024]{2,1,0:T(8,128)(2,1)} %param.13) | copy-start | bytes 1572868
  499.3 267.7 %reduce-scatter.11.cloned.1.call-start = ((), (), s32[]{:S(2)}) async-start(), calls=%async_computation.9 | async-start | bytes 1179648 | tf_op jit(solution)/shard_map/reduce_scatter | solution.py:75
Sparse Core Ops, SparseCore 0:
  24.7 72.2 all-gather.2
  120.8 218.4 reduce-scatter.4
  361.2 27.8 reduce-scatter.6
  406.4 72.2 all-gather.4
  499.5 218.4 reduce-scatter.8
  739.0 27.9 reduce-scatter.10
where the time goes:
time: 777 us; the launch traced here: 775 us
  waiting for transfers between devices  621 us (80%)
  blocking collectives  66 us (8%)
  local copies, waits for them, and re-layouts  41.5 us (5%)
  matrix products  21.4 us (3%)
  between operations  13.6 us (2%)
  other arithmetic  11.8 us (2%)
    reduce_scatter x2, waiting for transfers between devices, body(): lax.psum_scatter(attend_local(part_queries, part_history, user_lengths, c...  437 us
    all_gather x2, waiting for transfers between devices, body(): lax.all_gather(queries.reshape(tok_rows, head_width), 'cache', axis=0, ti...  128 us
    reduce_scatter x2, waiting for transfers between devices, body(): lax.psum_scatter(branch_terms, 'head', scatter_dimension=1, tiled=True)  55.9 us
    psum x2, blocking collectives, body(): lax.psum((jnp.sum(attended, axis=1), jnp.sum(attended * attended, axis=1)...  35.3 us
    all_gather x2, blocking collectives, body(): lax.all_gather(hidden, 'head', axis=1, tiled=True)  30.7 us
    unnamed x14, local copies, waits for them, and re-layouts  17.9 us
    dot_general x2, matrix products, attend_local(): jnp.einsum('rhce,rehd->rchd', weights, blocks[:, :, :, 1, :], preferred_e...  17.1 us
  transfers between devices with their start and end apart: 6, of which 6 were waited for; matrix products, arithmetic and copies ran while one was open for 2% of the time, Pallas kernels for 0%

commit v1 on v0

v1 whole, which is shorter than its diff:
```python
import functools

import jax
import jax.numpy as jnp
from jax import lax
from jax.experimental import pallas as pl
from jax.experimental.pallas import tpu as pltpu
from jax.sharding import PartitionSpec as P

DH = 64
LAYERS = 2
LANES = 128
X_SIZE = 4
CORES = 2
EXTRA = 16
MESH = pl.DeviceIdType.MESH
F32 = jnp.float32
BF16 = jnp.bfloat16


def dot(a, b, dims=((1,), (0,))):
    return lax.dot_general(a, b, (dims, ((), ())), preferred_element_type=F32)


def silu(v):
    half = v * 0.5
    return half + half * jnp.tanh(half)


def lane_halves(rows):
    return lax.broadcasted_iota(jnp.int32, (rows, LANES), 1) < DH


def head_rows(value, dtype):
    row = lax.broadcasted_iota(jnp.int32, (8, LANES), 0)
    lane = lax.broadcasted_iota(jnp.int32, (8, LANES), 1)
    own = ((row == 0) & (lane < DH)) | ((row == 1) & (lane >= DH))
    return jnp.where(own, value, 0.0).astype(dtype)


def spread(packed):
    flat = jnp.concatenate([packed[0:8], packed[8:16]], axis=1)
    return dot(flat.astype(BF16), head_rows(1.0, BF16), ((0,), (0,)))


def centre(block):
    flat = dot(head_rows(1.0 / DH, BF16), block.astype(BF16), ((1,), (1,)))
    packed = jnp.concatenate([flat[:, 0:LANES], flat[:, LANES:]], axis=0)
    return packed.astype(BF16).astype(F32)


def kernel(
    sizes, req_ref, len_ref, tok_hbm, hist_hbm, w_in_hbm, w_out_hbm, out_ref,
    hist0, hist1, kvs, kvr, hid, hid_f, w_in, wo0, wo_own, wo1, q_all, gate_all, part_s, part_r, att_all,
    load_sem, tok_s, tok_r, kv_s, kv_r, q_s, q_r, g_s, g_r, p_s, p_r, a_s, a_r, wo_s, wo_r, wt_s, wt_r,
):
    nz, nx, nh = sizes
    hists = (hist0, hist1)
    users, events = hist0.shape[0], hist0.shape[1]
    rows = hid.shape[1]
    cache, head = lax.axis_index("cache"), lax.axis_index("head")
    z, x = cache // nx, cache % nx
    core = head % CORES

    def z_peer(d):
        return (((z + d) % nz) * nx + x, head)

    def x_peer(d):
        return (z * nx + (x + d) % nx, head)

    def h_peer(d):
        return (cache, (head + d) % nh)

    def remote(src, dst, send, recv, device):
        return pltpu.make_async_remote_copy(
            src_ref=src, dst_ref=dst, send_sem=send, recv_sem=recv, device_id=device, device_id_type=MESH
        )

    def distance(i):
        return nz // 2 + (1 - 2 * (i % 2)) * ((i + 1) // 2)

    loads = [
        pltpu.make_async_copy(hist_hbm.at[0], hist0, load_sem.at[0]),
        pltpu.make_async_copy(tok_hbm, hid.at[head], load_sem.at[1]),
        pltpu.make_async_copy(w_in_hbm, w_in, load_sem.at[2]),
        pltpu.make_async_copy(w_out_hbm, wo_own, load_sem.at[3]),
        pltpu.make_async_copy(hist_hbm.at[1], hist1, load_sem.at[4]),
    ]
    for load in loads:
        load.start()

    barrier = pltpu.get_barrier_semaphore()
    peers = (
        [z_peer(d) for d in range(1, nz)] + [x_peer(d) for d in range(1, nx)] + [h_peer(d) for d in range(1, nh)]
    )
    for peer in peers:
        pl.semaphore_signal(barrier, inc=1, device_id=peer, device_id_type=MESH)

    def prepare(layer):
        hist = hists[layer]

        def one(u, carry):
            live = len_ref[u] - cache * events
            mask = lax.broadcasted_iota(jnp.int32, (events, LANES), 0) < live
            left = pltpu.roll(hist[u, :, 0:LANES].astype(F32), DH, 1)
            right = hist[u, :, LANES : 2 * LANES].astype(F32)
            hist[u, :, 0:LANES] = jnp.where(mask, left, 0.0).astype(BF16)
            hist[u, :, LANES : 2 * LANES] = jnp.where(mask, right, 0.0).astype(BF16)
            return carry

        lax.fori_loop(0, users, one, 0)

    def gather(layer):
        def one(i, carry):
            z_to = (z + distance(i)) % nz
            for d in range(nx):
                block = hists[layer][req_ref[z_to * nx + (x + d) % nx, 0]]
                if d == 0:
                    kvr[layer, z_to, pl.ds(x * events, events)] = block
                else:
                    kvs[layer, i, d - 1] = block
            return carry

        lax.fori_loop(0, nz, one, 0)

    def kv_copy(layer, i, d):
        z_to = (z + distance(i)) % nz
        return remote(
            kvs.at[layer, i, d - 1], kvr.at[layer, z_to, pl.ds(x * events, events)],
            kv_s.at[layer, i, d - 1], kv_r.at[layer, i, d - 1], x_peer(d),
        )

    def kv_send(layer, i):
        for d in range(1, nx):
            kv_copy(layer, i, d).start()

    def tok_copy(d):
        return remote(hid.at[head], hid.at[head], tok_s.at[d - 1], tok_r.at[d - 1], h_peer(d))

    def wo_peer(d):
        return (cache, (head + CORES * d) % nh)

    def sibling():
        return (cache, head + 1 - 2 * core)

    def wo_copy(d):
        return remote(wo0.at[head], wo0.at[head], wo_s.at[d], wo_r.at[d], wo_peer(d) if d else sibling())

    def wo_forward(d):
        src = (head + nh - CORES * d) % nh
        return remote(wo0.at[src], wo0.at[src], wo_s.at[nh + d], wo_r.at[nh + d], sibling())

    def wt_copy(d):
        to = (head + d) % nh
        return remote(
            wo1.at[1, to], wo1.at[0, head], wt_s.at[d - 1], wt_r.at[d - 1], h_peer(d)
        )

    def q_copy(layer, d):
        return remote(q_all.at[layer, z], q_all.at[layer, z], q_s.at[layer, d], q_r.at[layer, d], z_peer(d))

    def gate_copy(layer, d):
        return remote(
            gate_all.at[layer, head], gate_all.at[layer, head], g_s.at[layer, d - 1], g_r.at[layer, d - 1], h_peer(d)
        )

    def part_copy(layer, i):
        return remote(
            part_s.at[layer, i], part_r.at[layer, i], p_s.at[layer, i], p_r.at[layer, i], z_peer(distance(i))
        )

    def att_copy(layer, d):
        return remote(
            att_all.at[layer, head], att_all.at[layer, head], a_s.at[layer, d - 1], a_r.at[layer, d - 1], h_peer(d)
        )

    loads[0].wait()
    prepare(0)
    gather(0)
    pl.semaphore_wait(barrier, len(peers))
    loads[1].wait()
    for d in range(1, nh):
        tok_copy(d).start()
    lax.fori_loop(0, nz, lambda i, c: (kv_send(0, i), c)[1], 0)

    loads[3].wait()
    wo0[head] = wo_own[0]
    for d in range(nh // CORES):
        wo_copy(d).start()
    for b in range(nh):
        wo1[1, b] = wo_own[1, :, b * LANES : (b + 1) * LANES]
    wo1[0, head] = wo1[1, head]
    for d in range(1, nh):
        wt_copy(d).start()

    loads[4].wait()
    prepare(1)
    gather(1)

    def project(layer):
        if layer == 0:
            for d in range(1, nh):
                tok_copy(d).wait_recv()
            loads[2].wait()
        hidden = jnp.concatenate([hid[b] for b in range(nh)], axis=1)
        left = silu(dot(hidden, w_in[layer, :, 0:LANES]))
        right = pltpu.roll(silu(dot(hidden, w_in[layer, :, LANES : 2 * LANES])), DH, 1)
        low = lane_halves(rows)
        q_all[layer, z] = (jnp.where(low, right, left).astype(BF16).astype(F32) * (0.5 * DH**-0.5)).astype(BF16)
        gate_all[layer, head] = jnp.where(low, left, right).astype(BF16)
        for i in range(nz - 1):
            q_copy(layer, distance(i)).start()
        for d in range(1, nh):
            gate_copy(layer, d).start()

    def attend(layer, z_of):
        q = q_all[layer, z_of]
        low = lane_halves(rows)
        zero = jnp.zeros_like(q)
        outs = []
        for local, q_one in ((0, jnp.where(low, zero, q)), (1, jnp.where(low, q, zero))):
            total = None
            for at in range(0, nx * events, 256):
                kv = kvr[layer, z_of, at : at + 256, local * LANES : (local + 1) * LANES]
                s = dot(q_one, kv, ((1,), (1,)))
                w = (s + s * jnp.tanh(s)).astype(BF16)
                o = dot(w, kv)
                total = o if total is None else total + o
            outs.append(total)
        block = jnp.where(low, outs[0], outs[1])
        centres = centre(block)
        return block - spread(centres), centres

    def attention(layer):
        def one(i, carry):
            d = distance(i)
            q_copy(layer, nz - d).wait_recv()
            for e in range(1, nx):
                kv_copy(layer, i, e).wait_recv()
            block, centres = attend(layer, (z + d) % nz)
            part_s[layer, i, 0:rows] = block.astype(BF16)
            part_s[layer, i, rows : rows + EXTRA] = centres.astype(BF16)
            part_copy(layer, i).start()
            if layer == 0:
                kv_send(1, i)
            return carry

        lax.fori_loop(0, nz - 1, one, 0)
        for e in range(1, nx):
            kv_copy(layer, nz - 1, e).wait_recv()
        if layer == 0:
            kv_send(1, nz - 1)
        block, centres = attend(layer, z)

        def add(i, carry):
            part_copy(layer, i).wait_recv()
            return (
                carry[0] + part_r[layer, i, 0:rows].astype(F32),
                carry[1] + part_r[layer, i, rows : rows + EXTRA].astype(F32),
            )

        for i in range(nz - 1):
            block, centres = add(i, (block, centres))
        high = centres.astype(BF16)
        att_all[layer, head, 0:rows] = block.astype(BF16)
        att_all[layer, head, rows : rows + EXTRA] = high
        att_all[layer, head, rows + EXTRA : rows + 2 * EXTRA] = (centres - high.astype(F32)).astype(BF16)
        for d in range(1, nh):
            att_copy(layer, d).start()

    def normed(layer):
        total = jnp.zeros((rows, LANES), F32)
        squares = jnp.zeros((rows, LANES), F32)
        for d in range(1, nh):
            gate_copy(layer, d).wait_recv()
            att_copy(layer, d).wait_recv()
        for b in range(nh):
            block = (
                att_all[layer, b, 0:rows].astype(F32)
                + spread(att_all[layer, b, rows : rows + EXTRA].astype(F32))
                + spread(att_all[layer, b, rows + EXTRA : rows + 2 * EXTRA].astype(F32))
            )
            hid_f[b] = block
            total = total + block
            squares = squares + block * block
        width = nh * LANES
        mean = jnp.sum(total, axis=1, keepdims=True) * (1.0 / width)
        var = jnp.sum(squares, axis=1, keepdims=True) * (1.0 / width) - mean * mean
        scale = lax.rsqrt(var + 1e-05)
        return jnp.concatenate(
            [((hid_f[b] - mean) * scale * gate_all[layer, b].astype(F32)).astype(BF16) for b in range(nh)], axis=1
        )

    project(0)
    attention(0)
    wo_copy(0).wait_recv()
    for d in range(1, nh // CORES):
        wo_copy(d).wait_recv()
        wo_forward(d).start()
    for d in range(1, nh // CORES):
        wo_forward(d).wait_recv()
    gated = normed(0)
    for d in range(1, nh):
        tok_copy(d).wait_send()
    full = wo0[...].reshape(nh * LANES, nh * LANES)
    for b in range(nh):
        branch = dot(gated, full[:, b * LANES : (b + 1) * LANES])
        hid[b] = (hid[b].astype(F32) + branch).astype(BF16)
    project(1)
    attention(1)
    for d in range(1, nh):
        wt_copy(d).wait_recv()
    gated = normed(1)
    branch = dot(gated, wo1[0].reshape(nh * LANES, LANES))
    out_ref[...] = (hid[head].astype(F32) + branch).astype(BF16)

    for d in range(1, nh):
        wt_copy(d).wait_send()
    for d in range(nh // CORES):
        wo_copy(d).wait_send()
        if d:
            wo_forward(d).wait_send()
    for layer in range(LAYERS):
        for d in range(1, nh):
            gate_copy(layer, d).wait_send()
            att_copy(layer, d).wait_send()

        def finish(i, carry):
            q_copy(layer, distance(i)).wait_send()
            part_copy(layer, i).wait_send()
            for d in range(1, nx):
                kv_copy(layer, i, d).wait_send()
            return carry

        lax.fori_loop(0, nz - 1, finish, 0)
        for d in range(1, nx):
            kv_copy(layer, nz - 1, d).wait_send()


def body(x_size, nc, nh, tokens, request_user, hist_len, history, w_in, w_out):
    nx = x_size
    nz = nc // nx
    rows = tokens.shape[0]
    users, events = history.shape[1], history.shape[2]
    width = nh * LANES
    any_ref = pl.BlockSpec(memory_space=pl.ANY)
    smem = pl.BlockSpec(memory_space=pltpu.SMEM)
    sem = pltpu.SemaphoreType.DMA
    return pl.pallas_call(
        functools.partial(kernel, (nz, nx, nh)),
        out_shape=jax.ShapeDtypeStruct((rows, LANES), BF16),
        in_specs=[smem, smem, any_ref, any_ref, any_ref, any_ref],
        out_specs=pl.BlockSpec(memory_space=pltpu.VMEM),
        scratch_shapes=[
            pltpu.VMEM((users, events, 2 * LANES), BF16),
            pltpu.VMEM((users, events, 2 * LANES), BF16),
            pltpu.VMEM((LAYERS, nz, nx - 1, events, 2 * LANES), BF16),
            pltpu.VMEM((LAYERS, nz, nx * events, 2 * LANES), BF16),
            pltpu.VMEM((nh, rows, LANES), BF16),
            pltpu.VMEM((nh, rows, LANES), F32),
            pltpu.VMEM((LAYERS, width, 2 * LANES), BF16),
            pltpu.VMEM((nh, LANES, width), BF16),
            pltpu.VMEM((LAYERS, LANES, width), BF16),
            pltpu.VMEM((2, nh, LANES, LANES), BF16),
            pltpu.VMEM((LAYERS, nz, rows, LANES), BF16),
            pltpu.VMEM((LAYERS, nh, rows, LANES), BF16),
            pltpu.VMEM((LAYERS, nz, rows + EXTRA, LANES), BF16),
            pltpu.VMEM((LAYERS, nz, rows + EXTRA, LANES), BF16),
            pltpu.VMEM((LAYERS, nh, rows + 2 * EXTRA, LANES), BF16),
            sem((5,)),
            sem((nh,)), sem((nh,)),
            sem((LAYERS, nz, nx)), sem((LAYERS, nz, nx)),
            sem((LAYERS, nz)), sem((LAYERS, nz)),
            sem((LAYERS, nh)), sem((LAYERS, nh)),
            sem((LAYERS, nz)), sem((LAYERS, nz)),
            sem((LAYERS, nh)), sem((LAYERS, nh)),
            sem((2 * nh,)), sem((2 * nh,)),
            sem((nh,)), sem((nh,)),
        ],
        compiler_params=pltpu.CompilerParams(
            collective_id=0, has_side_effects=True, vmem_limit_bytes=48 * 1024 * 1024
        ),
    )(request_user, hist_len, tokens, history, w_in, w_out)


def solution(mesh):
    in_specs = (
        P("cache", "head"),
        P(),
        P(),
        P(None, None, "cache", "head"),
        P(None, None, "head"),
        P(None, "head", None),
    )
    run = functools.partial(body, X_SIZE, mesh.shape["cache"], mesh.shape["head"])
    return jax.shard_map(run, mesh=mesh, in_specs=in_specs, out_specs=P("cache", "head"), check_vma=False)
```

time: 777 us -> 102 us (0.13)
  waiting for transfers between devices: 621 us -> 0 us
  Pallas kernels: 0 us -> 94.5 us
  blocking collectives: 66 us -> 0 us
  local copies, waits for them, and re-layouts: 41.5 us -> 6.72 us
  matrix products: 21.4 us -> 0 us
  between operations: 13.6 us -> 0.01 us
  other arithmetic: 11.8 us -> 0 us
    reduce_scatter x4 -> x0, waiting for transfers between devices: 493 us -> none  [the longest x2 437 us: body(): lax.psum_scatter(attend_local(part_queries, part_history, user_lengths, c...]
    all_gather x2 -> x0, waiting for transfers between devices: 128 us -> none  [body(): lax.all_gather(queries.reshape(tok_rows, head_width), 'cache', axis=0, ti...]
    pallas_call x0 -> x1, Pallas kernels: none -> 94.5 us  [body(): pl.pallas_call(functools.partial(kernel, (nz, nx, nh)), out_shape=jax.Sha...]
    psum x2 -> x0, blocking collectives: 35.3 us -> none  [body(): lax.psum((jnp.sum(attended, axis=1), jnp.sum(attended * attended, axis=1)...]
    all_gather x2 -> x0, blocking collectives: 30.7 us -> none  [body(): lax.all_gather(hidden, 'head', axis=1, tiled=True)]
    dot_general x6 -> x0, matrix products: 21.4 us -> none  [the longest x2 17.1 us: attend_local(): jnp.einsum('rhce,rehd->rchd', weights, blocks[:, :, :, 1, :], preferred_e...]
    unnamed x14 -> x12, local copies, waits for them, and re-layouts: 17.9 us -> 6.72 us
    transpose x2 -> x0, local copies, waits for them, and re-layouts: 9.23 us -> none  [attend_local(): jnp.einsum('rhce,rehd->rchd', weights, blocks[:, :, :, 1, :], preferred_e...]
  transfers between devices with their start and end apart: 6 -> 0, of which waited for: 6 -> 0; matrix products, arithmetic and copies ran while one was open for 2% -> 0% of each run, Pallas kernels for 0% -> 0%
where the time goes in v1:
time: 102 us; the launch traced here: 101 us
  Pallas kernels  94.5 us (93%)
  local copies, waits for them, and re-layouts  6.72 us (7%)
    pallas_call x1, Pallas kernels, body(): pl.pallas_call(functools.partial(kernel, (nz, nx, nh)), out_shape=jax.Sha...  94.5 us
    unnamed x12, local copies, waits for them, and re-layouts  6.72 us

profile of v1, /device:TPU:1, one launch (start us, length us, event | category | flops | bytes accessed | tf_op | source)
XLA Modules:
  0.0 101.3 jit_solution(427778207379544867)
XLA Ops:
  0.0 0.7 copy.7.req_ref
  0.7 0.0 copy-start
  0.7 1.6 %copy-done = bf16[2,16,128,256]{3,2,1,0:T(8,128)(2,1)S(1)} copy-done((bf16[2,16,128,256]{3,2,1,0:T(8,128)(2,1)S(1)}, bf16[2,16,128,256]{3,2,1,0:T(8,128)(2,1)}, u32[]{:S(2)}) %copy-start) | copy-done | bytes 2097176
  2.3 0.0 copy-start.1
  2.3 1.2 %copy-done.1 = bf16[2,1024,256]{2,1,0:T(8,128)(2,1)S(1)} copy-done((bf16[2,1024,256]{2,1,0:T(8,128)(2,1)S(1)}, bf16[2,1024,256]{2,1,0:T(8,128)(2,1)}, u32[]{:S(2)}) %copy-start.1) | copy-done | bytes 1048600
  3.6 0.0 copy-start.2
  3.6 1.0 %copy-done.2 = bf16[2,128,1024]{2,1,0:T(8,128)(2,1)S(1)} copy-done((bf16[2,128,1024]{2,1,0:T(8,128)(2,1)S(1)}, bf16[2,128,1024]{2,1,0:T(8,128)(2,1)}, u32[]{:S(2)}) %copy-start.2) | copy-done | bytes 524312
  4.6 0.0 copy-start.3
  4.6 0.8 copy-done.3
  5.4 0.0 copy-start.4
  5.4 0.7 copy-done.4
  6.1 94.5 %shard_map.64 = bf16[256,128]{1,0:T(8,128)(2,1)S(1)} custom-call(s32[32,1]{1,0:T(8,128)S(1)} %copy.7.req_ref, s32[16]{0:T(128)S(1)} %copy-done.4, bf16[256,128]{1,0:T(8,128)(2,1)S(1)} %copy-done.3, bf16[2,16,128,256]{3,2,1,0:T(8,128)(2,1)S(1)} %copy-done, bf16[2,1024,256]{2,1,0:T(8,128)(2,1)S(1)} %copy-done.1, bf16[2,128,1024]{2,1,0:T(8,128)(2,1)S(1)} %copy-done.2), custom_call_target="tpu_custom_call" | custom-call | tf_op jit(solution)/shard_map/pallas_call | solution.py:349
  100.6 0.6 copy.9
Async XLA Ops:
  0.7 1.6 %copy-start = (bf16[2,16,128,256]{3,2,1,0:T(8,128)(2,1)S(1)}, bf16[2,16,128,256]{3,2,1,0:T(8,128)(2,1)}, u32[]{:S(2)}) copy-start(bf16[2,16,128,256]{3,2,1,0:T(8,128)(2,1)} %hist_hbm.1) | copy-start | bytes 6291460
  2.3 1.2 %copy-start.1 = (bf16[2,1024,256]{2,1,0:T(8,128)(2,1)S(1)}, bf16[2,1024,256]{2,1,0:T(8,128)(2,1)}, u32[]{:S(2)}) copy-start(bf16[2,1024,256]{2,1,0:T(8,128)(2,1)} %w_in_hbm.1) | copy-start | bytes 3145732
  3.6 1.0 %copy-start.2 = (bf16[2,128,1024]{2,1,0:T(8,128)(2,1)S(1)}, bf16[2,128,1024]{2,1,0:T(8,128)(2,1)}, u32[]{:S(2)}) copy-start(bf16[2,128,1024]{2,1,0:T(8,128)(2,1)} %w_out_hbm.1) | copy-start | bytes 1572868
  4.6 0.8 copy-start.3
  5.4 0.7 copy-start.4

commit v2 on v0

v2 whole, which is shorter than its diff:
```python
import functools

import jax
import jax.numpy as jnp
from jax import lax
from jax.experimental import pallas as pl
from jax.experimental.pallas import tpu as pltpu
from jax.sharding import PartitionSpec as P

DH = 64
LAYERS = 2
LANES = 128
X_SIZE = 4
CORES = 2
EXTRA = 16
MESH = pl.DeviceIdType.MESH
F32 = jnp.float32
BF16 = jnp.bfloat16


def dot(a, b, dims=((1,), (0,))):
    return lax.dot_general(a, b, (dims, ((), ())), preferred_element_type=F32)


def silu(v):
    half = v * 0.5
    return half + half * jnp.tanh(half)


def lane_halves(rows):
    return lax.broadcasted_iota(jnp.int32, (rows, LANES), 1) < DH


def head_rows(value, dtype):
    row = lax.broadcasted_iota(jnp.int32, (8, LANES), 0)
    lane = lax.broadcasted_iota(jnp.int32, (8, LANES), 1)
    own = ((row == 0) & (lane < DH)) | ((row == 1) & (lane >= DH))
    return jnp.where(own, value, 0.0).astype(dtype)


def spread(flat):
    pick = head_rows(1.0, F32)
    if flat.shape[0] == 16:
        pick = jnp.concatenate([pick, pick], axis=0)
    return dot(flat, pick.astype(BF16), ((0,), (0,)))


def centre(block):
    return dot(head_rows(1.0 / DH, BF16), block.astype(BF16), ((1,), (1,))).astype(BF16)


def kernel(
    sizes, req_ref, len_ref, tok_hbm, hist_hbm, w_in_hbm, w_out_hbm, out_ref,
    raw0, raw1, hist0, hist1, stay_s, stay, pair_s, pair, tok, hid, hid_f, w_in, wo0, wo_own, wo1_s, wo1,
    q_all, gate_s, gate_all, part_s, part_r, att_s, att_all, last_s, last_r,
    load_sem, tok_sem, stay_ss, stay_rs, pair_ss, pair_rs, q_ss, q_rs, p_ss, p_rs, g_ss, g_rs, a_ss, a_rs, wo_sem, wt_sem,
    hid_sem, last_sem,
):
    nz, nx, nh = sizes
    steps = nz // 2
    users, events = raw0.shape[0], raw0.shape[1]
    rows = tok.shape[1]
    half = rows // CORES
    raws, hists = (raw0, raw1), (hist0, hist1)
    cache, head = lax.axis_index("cache"), lax.axis_index("head")
    z, x = cache // nx, cache % nx
    chip, core = head // CORES, head % CORES
    own_rows = pl.ds(pl.multiple_of(core * half, half), half)
    other_rows = pl.ds(pl.multiple_of((1 - core) * half, half), half)
    side = 1 - 2 * (z % 2)
    groups = ((0, 1, 2, 3), (0, 2)) if steps == 4 else (tuple(range(steps)), tuple(range(steps)))
    spans = [steps // len(g) for g in groups]

    def at(d_z, d_x):
        return (((z + d_z + nz) % nz) * nx + (x + d_x) % nx, head)

    def h_peer(d):
        return (cache, (head + d) % nh)

    sibling = (cache, head + 1 - 2 * core)

    def remote(src, dst, send, recv, device):
        return pltpu.make_async_remote_copy(
            src_ref=src, dst_ref=dst, send_sem=send, recv_sem=recv, device_id=device, device_id_type=MESH
        )

    def drain(ref, sem):
        pltpu.make_async_copy(ref, ref, sem).wait()

    loads = [
        pltpu.make_async_copy(hist_hbm.at[0], raw0, load_sem.at[0]),
        pltpu.make_async_copy(tok_hbm, tok.at[head], load_sem.at[1]),
        pltpu.make_async_copy(hist_hbm.at[1], raw1, load_sem.at[2]),
        pltpu.make_async_copy(w_in_hbm, w_in, load_sem.at[3]),
        pltpu.make_async_copy(w_out_hbm, wo_own, load_sem.at[4]),
    ]
    for load in loads:
        load.start()

    barrier = pltpu.get_barrier_semaphore()
    peers = [at(0, d) for d in range(1, nx)] + [h_peer(d) for d in range(1, nh)]
    peers += [at(2 * k, 0) for k in range(1, steps)]
    peers += [at(s, d) for s in (1, -1) for d in range(nx)]
    for peer in peers:
        pl.semaphore_signal(barrier, inc=1, device_id=peer, device_id_type=MESH)

    def prepare(layer):
        def one(u, carry):
            live = len_ref[u] - cache * events
            mask = lax.broadcasted_iota(jnp.int32, (events, LANES), 0) < live
            left = pltpu.roll(raws[layer][u, :, 0:LANES].astype(F32), DH, 1)
            right = raws[layer][u, :, LANES : 2 * LANES].astype(F32)
            hists[layer][u, 0] = jnp.where(mask, left, 0.0).astype(BF16)
            hists[layer][u, 1] = jnp.where(mask, right, 0.0).astype(BF16)
            return carry

        lax.fori_loop(0, users, one, 0)

    def gather(layer):
        def one(k, carry):
            for d in range(nx):
                to_x = (x + d) % nx
                block = hists[layer][req_ref[((z + 2 * k) % nz) * nx + to_x]]
                if d == 0:
                    stay[layer, x, k] = block
                else:
                    stay_s[layer, d - 1, k] = block
                for j in range(2):
                    to_z = (z + side * (1 - 2 * j) + 2 * k + nz) % nz
                    pair_s[layer, d, j, k] = hists[layer][req_ref[to_z * nx + to_x], j]
            return carry

        lax.fori_loop(0, steps, one, 0)

    def kv_send(layer, g):
        span = pl.ds(g, spans[layer])
        for d in range(nx):
            for j in range(2):
                remote(
                    pair_s.at[layer, d, j, span], pair.at[layer, x, j, span],
                    pair_ss.at[layer], pair_rs.at[layer, g], at(side * (1 - 2 * j), d),
                ).start()
            if d:
                remote(
                    stay_s.at[layer, d - 1, span], stay.at[layer, x, span],
                    stay_ss.at[layer], stay_rs.at[layer, g], at(0, d),
                ).start()

    def kv_wait(layer, g):
        span = pl.ds(g, spans[layer])
        drain(stay.at[layer, 0 : nx - 1, span], stay_rs.at[layer, g])
        drain(pair.at[layer, :, :, span], pair_rs.at[layer, g])

    loads[0].wait()
    prepare(0)
    gather(0)
    loads[1].wait()
    pl.semaphore_wait(barrier, len(peers))
    for d in range(1, nh):
        remote(tok.at[head], tok.at[head], tok_sem.at[0], tok_sem.at[1], h_peer(d)).start()
    for g in groups[0]:
        kv_send(0, g)
    loads[2].wait()
    prepare(1)
    gather(1)
    loads[3].wait()
    loads[4].wait()
    wo0[head] = wo_own[0]
    for b in range(nh):
        wo1_s[b // CORES, b % CORES] = wo_own[1, :, b * LANES : (b + 1) * LANES]
    wo1[head] = wo1_s[chip]
    drain(tok.at[0 : nh - 1], tok_sem.at[1])

    def project(layer, hidden, at_rows):
        count = hidden.shape[0]
        left = silu(dot(hidden, w_in[layer, :, 0:LANES]))
        right = pltpu.roll(silu(dot(hidden, w_in[layer, :, LANES : 2 * LANES])), DH, 1)
        low = lane_halves(count)
        q = (jnp.where(low, right, left).astype(BF16).astype(F32) * (0.5 * DH**-0.5)).astype(BF16)
        gates = jnp.where(low, left, right).astype(BF16)
        q_all[layer, 0, at_rows] = q
        return gates

    def send_projected(layer):
        for k in range(1, steps):
            remote(
                q_all.at[layer, 0], q_all.at[layer, steps - k], q_ss.at[layer], q_rs.at[layer, steps - k], at(2 * k, 0)
            ).start()
        gate_all[layer, head] = gate_s[layer, core]
        for d in range(1, nh):
            remote(
                gate_s.at[layer, (head + d) % CORES], gate_all.at[layer, head], g_ss.at[layer], g_rs.at[layer], h_peer(d)
            ).start()

    def attend(layer, k):
        q = q_all[layer, k]
        low = lane_halves(rows)
        zero = jnp.zeros_like(q)
        outs = []
        for j, q_one in ((0, jnp.where(low, zero, q)), (1, jnp.where(low, q, zero))):
            total = None
            for s in range(0, nx, 2):
                for keys in (stay[layer, s : s + 2, k, j], pair[layer, s : s + 2, j, k]):
                    kv = keys.reshape(2 * events, LANES)
                    t = dot(q_one, kv, ((1,), (1,)))
                    o = dot((t + t * jnp.tanh(t)).astype(BF16), kv)
                    total = o if total is None else total + o
            outs.append(total)
        block = jnp.where(low, outs[0], outs[1])
        centres = centre(block)
        centred = block - spread(centres)
        wide = centres.astype(F32)
        return centred, jnp.concatenate([wide[:, 0:half], wide[:, half:]], axis=0)

    def attention(layer):
        if 0 in groups[layer]:
            kv_wait(layer, 0)
        block, centres = attend(layer, 0)

        def one(k, carry):
            drain(q_all.at[layer, k], q_rs.at[layer, k])
            part, middle = attend(layer, k)
            part_s[layer, k - 1, 0:rows] = part.astype(BF16)
            part_s[layer, k - 1, rows : rows + EXTRA] = middle.astype(BF16)
            remote(
                part_s.at[layer, k - 1], part_r.at[layer, k - 1], p_ss.at[layer], p_rs.at[layer], at(2 * k, 0)
            ).start()
            return carry

        if layer == 0:
            for k in range(1, steps):
                kv_wait(layer, k)
                if k == steps - 1:
                    for g in groups[1]:
                        kv_send(1, g)
                one(k, 0)
            if steps == 1:
                for g in groups[1]:
                    kv_send(1, g)
        else:
            for k in range(1, steps):
                if k in groups[layer]:
                    kv_wait(layer, k)
                one(k, 0)
        if steps > 1:
            drain(part_r.at[layer], p_rs.at[layer])
        for k in range(steps - 1):
            block = block + part_r[layer, k, 0:rows].astype(F32)
            centres = centres + part_r[layer, k, rows : rows + EXTRA].astype(F32)
        for c in range(CORES):
            middle = centres[8 * c : 8 * c + 8]
            high = middle.astype(BF16).astype(F32)
            att_s[layer, c, 0:half] = block[c * half : (c + 1) * half].astype(BF16)
            att_s[layer, c, half : half + EXTRA] = jnp.concatenate([high, middle - high], axis=0).astype(BF16)
        for d in range(1, nh):
            remote(
                att_s.at[layer, (head + d) % CORES], att_all.at[layer, head], a_ss.at[layer], a_rs.at[layer], h_peer(d)
            ).start()
        att_all[layer, head] = att_s[layer, core]

    def normed(layer):
        total = jnp.zeros((half, LANES), F32)
        squares = jnp.zeros((half, LANES), F32)
        drain(gate_all.at[layer, 0 : nh - 1], g_rs.at[layer])
        drain(att_all.at[layer, 0 : nh - 1], a_rs.at[layer])
        for b in range(nh):
            block = att_all[layer, b, 0:half].astype(F32) + spread(att_all[layer, b, half : half + EXTRA])
            hid_f[b] = block
            total = total + block
            squares = squares + block * block
        width = nh * LANES
        mean = jnp.sum(total, axis=1, keepdims=True) * (1.0 / width)
        var = jnp.sum(squares, axis=1, keepdims=True) * (1.0 / width) - mean * mean
        scale = lax.rsqrt(var + 1e-05)
        return jnp.concatenate(
            [((hid_f[b] - mean) * scale * gate_all[layer, b].astype(F32)).astype(BF16) for b in range(nh)], axis=1
        )

    gates = project(0, jnp.concatenate([tok[b] for b in range(nh)], axis=1), pl.ds(0, rows))
    for c in range(CORES):
        gate_s[0, c] = gates[c * half : (c + 1) * half]
    send_projected(0)
    for d in range(1, nh // CORES):
        remote(wo0.at[head], wo0.at[head], wo_sem.at[0], wo_sem.at[1], h_peer(CORES * d)).start()
    remote(wo0.at[head], wo0.at[head], wo_sem.at[0], wo_sem.at[2], sibling).start()
    for d in range(1, nh):
        remote(wo1_s.at[((head + d) % nh) // CORES], wo1.at[head], wt_sem.at[0], wt_sem.at[1], h_peer(d)).start()
    attention(0)
    if nh > CORES:
        drain(wo0.at[0 : nh // CORES - 1], wo_sem.at[1])
    for d in range(1, nh // CORES):
        src = (head + CORES * d) % nh
        remote(wo0.at[src], wo0.at[src], wo_sem.at[0], wo_sem.at[2], sibling).start()
    drain(wo0.at[0 : nh // CORES], wo_sem.at[2])
    gated = normed(0)
    full = wo0[...].reshape(nh * LANES, nh * LANES)
    for b in range(0, nh, 2):
        branch = dot(gated, full[:, b * LANES : (b + 2) * LANES])
        for e in range(2):
            hid[core, b + e] = (
                tok[b + e, own_rows].astype(F32) + branch[:, e * LANES : (e + 1) * LANES]
            ).astype(BF16)
        remote(hid.at[core, b : b + 2], hid.at[core, b : b + 2], hid_sem.at[0], hid_sem.at[1], sibling).start()
    gate_s[1, core] = project(1, jnp.concatenate([hid[core, b] for b in range(nh)], axis=1), own_rows)
    drain(hid.at[0], hid_sem.at[1])
    gate_s[1, 1 - core] = project(1, jnp.concatenate([hid[1 - core, b] for b in range(nh)], axis=1), other_rows)
    send_projected(1)
    attention(1)
    drain(wo1.at[0 : nh - 1], wt_sem.at[1])
    gated = normed(1)

    def final(c):
        branch = dot(gated, wo1[:, c].reshape(nh * LANES, LANES))
        return (hid[core, chip * CORES + c].astype(F32) + branch).astype(BF16)

    last_s[...] = final(1 - core)
    remote(last_s, last_r, last_sem.at[0], last_sem.at[1], sibling).start()
    out_ref[own_rows] = final(core)

    drain(tok.at[0 : nh - 1], tok_sem.at[0])
    drain(wo0.at[0 : nh - 1], wo_sem.at[0])
    drain(wo1.at[0 : nh - 1], wt_sem.at[0])
    drain(hid.at[0], hid_sem.at[0])
    for layer in range(LAYERS):
        drain(stay_s.at[layer], stay_ss.at[layer])
        drain(pair_s.at[layer], pair_ss.at[layer])
        if steps > 1:
            drain(q_all.at[layer, 0 : steps - 1], q_ss.at[layer])
            drain(part_s.at[layer], p_ss.at[layer])
        drain(gate_all.at[layer, 0 : nh - 1], g_ss.at[layer])
        drain(att_all.at[layer, 0 : nh - 1], a_ss.at[layer])
    drain(last_r, last_sem.at[1])
    drain(last_s, last_sem.at[0])
    out_ref[other_rows] = last_r[...]


def body(x_size, nc, nh, tokens, request_user, hist_len, history, w_in, w_out):
    nx = x_size
    nz = nc // nx
    steps = nz // 2
    rows = tokens.shape[0]
    half = rows // CORES
    users, events = history.shape[1], history.shape[2]
    width = nh * LANES
    hbm = pl.BlockSpec(memory_space=pltpu.HBM)
    smem = pl.BlockSpec(memory_space=pltpu.SMEM)
    sem = pltpu.SemaphoreType.DMA
    vmem = pltpu.VMEM
    return pl.pallas_call(
        functools.partial(kernel, (nz, nx, nh)),
        out_shape=jax.ShapeDtypeStruct((rows, LANES), BF16),
        in_specs=[smem, smem, hbm, hbm, hbm, hbm],
        out_specs=pl.BlockSpec(memory_space=pltpu.VMEM),
        scratch_shapes=[
            vmem((users, events, 2 * LANES), BF16),
            vmem((users, events, 2 * LANES), BF16),
            vmem((users, 2, events, LANES), BF16),
            vmem((users, 2, events, LANES), BF16),
            vmem((LAYERS, nx - 1, steps, 2, events, LANES), BF16),
            vmem((LAYERS, nx, steps, 2, events, LANES), BF16),
            vmem((LAYERS, nx, 2, steps, events, LANES), BF16),
            vmem((LAYERS, nx, 2, steps, events, LANES), BF16),
            vmem((nh, rows, LANES), BF16),
            vmem((CORES, nh, half, LANES), BF16),
            vmem((nh, half, LANES), F32),
            vmem((LAYERS, width, 2 * LANES), BF16),
            vmem((nh, LANES, width), BF16),
            vmem((LAYERS, LANES, width), BF16),
            vmem((nh // CORES, CORES, LANES, LANES), BF16),
            vmem((nh, CORES, LANES, LANES), BF16),
            vmem((LAYERS, steps, rows, LANES), BF16),
            vmem((LAYERS, CORES, half, LANES), BF16),
            vmem((LAYERS, nh, half, LANES), BF16),
            vmem((LAYERS, max(steps - 1, 1), rows + EXTRA, LANES), BF16),
            vmem((LAYERS, max(steps - 1, 1), rows + EXTRA, LANES), BF16),
            vmem((LAYERS, CORES, half + EXTRA, LANES), BF16),
            vmem((LAYERS, nh, half + EXTRA, LANES), BF16),
            vmem((half, LANES), BF16),
            vmem((half, LANES), BF16),
            sem((5,)),
            sem((2,)),
            sem((LAYERS,)), sem((LAYERS, steps)),
            sem((LAYERS,)), sem((LAYERS, steps)),
            sem((LAYERS,)), sem((LAYERS, steps)),
            sem((LAYERS,)), sem((LAYERS,)),
            sem((LAYERS,)), sem((LAYERS,)),
            sem((LAYERS,)), sem((LAYERS,)),
            sem((3,)), sem((2,)), sem((2,)), sem((2,)),
        ],
        compiler_params=pltpu.CompilerParams(
            collective_id=0, has_side_effects=True, vmem_limit_bytes=60 * 1024 * 1024
        ),
    )(request_user.reshape(-1), hist_len, tokens, history, w_in, w_out)


def solution(mesh):
    in_specs = (
        P("cache", "head"),
        P(),
        P(),
        P(None, None, "cache", "head"),
        P(None, None, "head"),
        P(None, "head", None),
    )
    run = functools.partial(body, X_SIZE, mesh.shape["cache"], mesh.shape["head"])
    return jax.shard_map(run, mesh=mesh, in_specs=in_specs, out_specs=P("cache", "head"), check_vma=False)
```

time: 777 us -> 89.8 us (0.12)
  waiting for transfers between devices: 621 us -> 0 us
  Pallas kernels: 0 us -> 88.2 us
  blocking collectives: 66 us -> 0 us
  local copies, waits for them, and re-layouts: 41.5 us -> 1.47 us
  matrix products: 21.4 us -> 0 us
  between operations: 13.6 us -> 0.01 us
  other arithmetic: 11.8 us -> 0 us
    reduce_scatter x4 -> x0, waiting for transfers between devices: 493 us -> none  [the longest x2 437 us: body(): lax.psum_scatter(attend_local(part_queries, part_history, user_lengths, c...]
    all_gather x2 -> x0, waiting for transfers between devices: 128 us -> none  [body(): lax.all_gather(queries.reshape(tok_rows, head_width), 'cache', axis=0, ti...]
    pallas_call x0 -> x1, Pallas kernels: none -> 88.2 us  [body(): pl.pallas_call(functools.partial(kernel, (nz, nx, nh)), out_shape=jax.Sha...]
    psum x2 -> x0, blocking collectives: 35.3 us -> none  [body(): lax.psum((jnp.sum(attended, axis=1), jnp.sum(attended * attended, axis=1)...]
    all_gather x2 -> x0, blocking collectives: 30.7 us -> none  [body(): lax.all_gather(hidden, 'head', axis=1, tiled=True)]
    dot_general x6 -> x0, matrix products: 21.4 us -> none  [the longest x2 17.1 us: attend_local(): jnp.einsum('rhce,rehd->rchd', weights, blocks[:, :, :, 1, :], preferred_e...]
    unnamed x14 -> x1, local copies, waits for them, and re-layouts: 17.9 us -> 1.47 us
    transpose x2 -> x0, local copies, waits for them, and re-layouts: 9.23 us -> none  [attend_local(): jnp.einsum('rhce,rehd->rchd', weights, blocks[:, :, :, 1, :], preferred_e...]
  transfers between devices with their start and end apart: 6 -> 0, of which waited for: 6 -> 0; matrix products, arithmetic and copies ran while one was open for 2% -> 0% of each run, Pallas kernels for 0% -> 0%
where the time goes in v2:
time: 89.8 us; the launch traced here: 89.6 us
  Pallas kernels  88.2 us (98%)
  local copies, waits for them, and re-layouts  1.47 us (2%)
    pallas_call x1, Pallas kernels, body(): pl.pallas_call(functools.partial(kernel, (nz, nx, nh)), out_shape=jax.Sha...  88.2 us

profile of v2, /device:TPU:1, one launch (start us, length us, event | category | flops | bytes accessed | tf_op | source)
XLA Modules:
  0.0 89.6 jit_solution(16354711916080516306)
XLA Ops:
  0.0 88.2 %shard_map.64 = bf16[256,128]{1,0:T(8,128)(2,1)} custom-call(s32[32]{0:T(128)} %bitcast.1, s32[16]{0:T(128)} %len_ref.1, bf16[256,128]{1,0:T(8,128)(2,1)} %tok_hbm.1, bf16[2,16,128,256]{3,2,1,0:T(8,128)(2,1)} %hist_hbm.1, bf16[2,1024,256]{2,1,0:T(8,128)(2,1)} %w_in_hbm.1, bf16[2,128,1024]{2,1,0:T(8,128)(2,1)} %w_out_hbm.1), custom_call_target="tpu_custom_call" | custom-call | tf_op jit(solution)/shard_map/pallas_call | solution.py:349
  88.2 1.5 %copy.8 = bf16[256,128]{1,0:T(8,128)(2,1)} copy(bf16[256,128]{1,0:T(8,128)(2,1)} %shard_map.64) | data formatting | bytes 131072

commit v3 on v2

--- a/solution.py
+++ b/solution.py
@@ -13,6 +13,7 @@
 X_SIZE = 4
 CORES = 2
 EXTRA = 16
+PACE = ((0, 1), (2, 3), (0, 1), (2,), (), (3,))
 MESH = pl.DeviceIdType.MESH
 F32 = jnp.float32
 BF16 = jnp.bfloat16
@@ -68,8 +69,6 @@
     own_rows = pl.ds(pl.multiple_of(core * half, half), half)
     other_rows = pl.ds(pl.multiple_of((1 - core) * half, half), half)
     side = 1 - 2 * (z % 2)
-    groups = ((0, 1, 2, 3), (0, 2)) if steps == 4 else (tuple(range(steps)), tuple(range(steps)))
-    spans = [steps // len(g) for g in groups]
 
     def at(d_z, d_x):
         return (((z + d_z + nz) % nz) * nx + (x + d_x) % nx, head)
@@ -133,7 +132,7 @@
         lax.fori_loop(0, steps, one, 0)
 
     def kv_send(layer, g):
-        span = pl.ds(g, spans[layer])
+        span = pl.ds(g, 1)
         for d in range(nx):
             for j in range(2):
                 remote(
@@ -146,8 +145,13 @@
                     stay_ss.at[layer], stay_rs.at[layer, g], at(0, d),
                 ).start()
 
+    def kv_batch(layer, batch):
+        for g in batch:
+            if g < steps:
+                kv_send(layer, g)
+
     def kv_wait(layer, g):
-        span = pl.ds(g, spans[layer])
+        span = pl.ds(g, 1)
         drain(stay.at[layer, 0 : nx - 1, span], stay_rs.at[layer, g])
         drain(pair.at[layer, :, :, span], pair_rs.at[layer, g])
 
@@ -158,8 +162,7 @@
     pl.semaphore_wait(barrier, len(peers))
     for d in range(1, nh):
         remote(tok.at[head], tok.at[head], tok_sem.at[0], tok_sem.at[1], h_peer(d)).start()
-    for g in groups[0]:
-        kv_send(0, g)
+    kv_batch(0, PACE[0])
     loads[2].wait()
     prepare(1)
     gather(1)
@@ -213,8 +216,7 @@
         return centred, jnp.concatenate([wide[:, 0:half], wide[:, half:]], axis=0)
 
     def attention(layer):
-        if 0 in groups[layer]:
-            kv_wait(layer, 0)
+        kv_wait(layer, 0)
         block, centres = attend(layer, 0)
 
         def one(k, carry):
@@ -227,21 +229,11 @@
             ).start()
             return carry
 
+        for k in range(1, steps):
+            kv_wait(layer, k)
+            one(k, 0)
         if layer == 0:
-            for k in range(1, steps):
-                kv_wait(layer, k)
-                if k == steps - 1:
-                    for g in groups[1]:
-                        kv_send(1, g)
-                one(k, 0)
-            if steps == 1:
-                for g in groups[1]:
-                    kv_send(1, g)
-        else:
-            for k in range(1, steps):
-                if k in groups[layer]:
-                    kv_wait(layer, k)
-                one(k, 0)
+            kv_batch(1, PACE[2])
         if steps > 1:
             drain(part_r.at[layer], p_rs.at[layer])
         for k in range(steps - 1):
@@ -257,6 +249,8 @@
                 att_s.at[layer, (head + d) % CORES], att_all.at[layer, head], a_ss.at[layer], a_rs.at[layer], h_peer(d)
             ).start()
         att_all[layer, head] = att_s[layer, core]
+        if layer == 0:
+            kv_batch(1, PACE[3])
 
     def normed(layer):
         total = jnp.zeros((half, LANES), F32)
@@ -280,6 +274,7 @@
     for c in range(CORES):
         gate_s[0, c] = gates[c * half : (c + 1) * half]
     send_projected(0)
+    kv_batch(0, PACE[1])
     for d in range(1, nh // CORES):
         remote(wo0.at[head], wo0.at[head], wo_sem.at[0], wo_sem.at[1], h_peer(CORES * d)).start()
     remote(wo0.at[head], wo0.at[head], wo_sem.at[0], wo_sem.at[2], sibling).start()
@@ -293,6 +288,7 @@
         remote(wo0.at[src], wo0.at[src], wo_sem.at[0], wo_sem.at[2], sibling).start()
     drain(wo0.at[0 : nh // CORES], wo_sem.at[2])
     gated = normed(0)
+    kv_batch(1, PACE[4])
     full = wo0[...].reshape(nh * LANES, nh * LANES)
     for b in range(0, nh, 2):
         branch = dot(gated, full[:, b * LANES : (b + 2) * LANES])
@@ -305,6 +301,7 @@
     drain(hid.at[0], hid_sem.at[1])
     gate_s[1, 1 - core] = project(1, jnp.concatenate([hid[1 - core, b] for b in range(nh)], axis=1), other_rows)
     send_projected(1)
+    kv_batch(1, PACE[5])
     attention(1)
     drain(wo1.at[0 : nh - 1], wt_sem.at[1])
     gated = normed(1)

time: 89.8 us -> 78.9 us (0.88)
  Pallas kernels: 88.2 us -> 77.3 us
    pallas_call x1, Pallas kernels: 88.2 us -> 77.3 us  [body(): pl.pallas_call(functools.partial(kernel, (nz, nx, nh)), out_shape=jax.Sha...]
where the time goes in v3:
time: 78.9 us; the launch traced here: 78.7 us
  Pallas kernels  77.3 us (98%)
  local copies, waits for them, and re-layouts  1.47 us (2%)
    pallas_call x1, Pallas kernels, body(): pl.pallas_call(functools.partial(kernel, (nz, nx, nh)), out_shape=jax.Sha...  77.3 us

profile of v3, /device:TPU:1, one launch (start us, length us, event | category | flops | bytes accessed | tf_op | source)
XLA Modules:
  0.0 78.7 jit_solution(11175506171976236306)
XLA Ops:
  0.0 77.3 %shard_map.64 = bf16[256,128]{1,0:T(8,128)(2,1)} custom-call(s32[32]{0:T(128)} %bitcast.1, s32[16]{0:T(128)} %len_ref.1, bf16[256,128]{1,0:T(8,128)(2,1)} %tok_hbm.1, bf16[2,16,128,256]{3,2,1,0:T(8,128)(2,1)} %hist_hbm.1, bf16[2,1024,256]{2,1,0:T(8,128)(2,1)} %w_in_hbm.1, bf16[2,128,1024]{2,1,0:T(8,128)(2,1)} %w_out_hbm.1), custom_call_target="tpu_custom_call" | custom-call | tf_op jit(solution)/shard_map/pallas_call | solution.py:346
  77.3 1.5 %copy.8 = bf16[256,128]{1,0:T(8,128)(2,1)} copy(bf16[256,128]{1,0:T(8,128)(2,1)} %shard_map.64) | data formatting | bytes 131072

commit v4 on v3

v4 whole, which is shorter than its diff:
```python
import functools

import jax
import jax.numpy as jnp
from jax import lax
from jax.experimental import pallas as pl
from jax.experimental.pallas import tpu as pltpu
from jax.sharding import PartitionSpec as P

DH = 64
LAYERS = 2
LANES = 128
X_SIZE = 4
CORES = 2
PARTS = 2
FIRST = (2, 1, 3)
ORDER = (((2, -1), (1, -1), (3, -1), (0, -1)), ((0, -1), (2, -1), (1, -1), (3, -1)))
EXTRA = 16
OWN, NEAR = True, False
PACE = (
    ((0, OWN, (2, 1, 3, 0)), (0, NEAR, (2, 1, 3, 0))), (),
    ((1, NEAR, (0, 2, 1, 3)), (1, OWN, (0, 2, 1, 3))), (), (), (),
)
MESH = pl.DeviceIdType.MESH
F32 = jnp.float32
BF16 = jnp.bfloat16


def dot(a, b, dims=((1,), (0,))):
    return lax.dot_general(a, b, (dims, ((), ())), preferred_element_type=F32)


def silu(v):
    half = v * 0.5
    return half + half * jnp.tanh(half)


def lane_halves(rows):
    return lax.broadcasted_iota(jnp.int32, (rows, LANES), 1) < DH


def head_rows(value, dtype):
    row = lax.broadcasted_iota(jnp.int32, (8, LANES), 0)
    lane = lax.broadcasted_iota(jnp.int32, (8, LANES), 1)
    own = ((row == 0) & (lane < DH)) | ((row == 1) & (lane >= DH))
    return jnp.where(own, value, 0.0).astype(dtype)


def spread(flat):
    pick = head_rows(1.0, F32)
    if flat.shape[0] == 16:
        pick = jnp.concatenate([pick, pick], axis=0)
    return dot(flat, pick.astype(BF16), ((0,), (0,)))


def centre(block):
    return dot(head_rows(1.0 / DH, BF16), block.astype(BF16), ((1,), (1,))).astype(BF16)


def kernel(
    sizes, req_ref, len_ref, tok_hbm, hist_hbm, w_in_hbm, w_out_hbm, out_ref,
    raw0, raw1, hist0, hist1, stay_s, stay, pair_s, pair, own_tok, hid0, hid, hid_f, w_in, wo0, wo_own, wo1_s, wo1,
    q_all, gate_s, gate_all, part_s, part_r, att_s, att_all, acc, mid, last_s, last_r,
    load_sem, tok_ss, tok_rs, fwd_ss, fwd_rs, stay_ss, stay_rs, pair_ss, pair_rs, q_ss, q_rs, p_ss, p_rs, g_ss, g_rs, a_ss, a_rs, wo_sem, wt_sem,
    hid_ss, hid_rs, last_sem,
):
    nz, nx, nh = sizes
    steps = nz // 2
    users, events = raw0.shape[0], raw0.shape[1]
    half = hid0.shape[3]
    rows = CORES * half
    raws, hists = (raw0, raw1), (hist0, hist1)
    cache, head = lax.axis_index("cache"), lax.axis_index("head")
    z, x = cache // nx, cache % nx
    chip, core = head // CORES, head % CORES
    side = 1 - 2 * (z % 2)

    def part_rows(p, c):
        return pl.ds(pl.multiple_of(p * rows + c * half, half), half)

    def at(d_z, d_x):
        return (((z + d_z + nz) % nz) * nx + (x + d_x) % nx, head)

    def h_peer(d):
        return (cache, (head + d) % nh)

    sibling = (cache, head + 1 - 2 * core)

    def remote(src, dst, send, recv, device):
        return pltpu.make_async_remote_copy(
            src_ref=src, dst_ref=dst, send_sem=send, recv_sem=recv, device_id=device, device_id_type=MESH
        )

    def drain(ref, sem):
        pltpu.make_async_copy(ref, ref, sem).wait()

    loads = [
        pltpu.make_async_copy(hist_hbm.at[0], raw0, load_sem.at[0]),
        pltpu.make_async_copy(tok_hbm, own_tok, load_sem.at[1]),
        pltpu.make_async_copy(hist_hbm.at[1], raw1, load_sem.at[2]),
        pltpu.make_async_copy(w_in_hbm, w_in, load_sem.at[3]),
        pltpu.make_async_copy(w_out_hbm, wo_own, load_sem.at[4]),
    ]
    for load in loads:
        load.start()

    barrier = pltpu.get_barrier_semaphore()
    peers = [at(0, d) for d in range(1, nx)] + [h_peer(d) for d in range(1, nh)]
    peers += [at(2 * k, 0) for k in range(1, steps)]
    peers += [at(s, d) for s in (1, -1) for d in range(nx)]
    for peer in peers:
        pl.semaphore_signal(barrier, inc=1, device_id=peer, device_id_type=MESH)

    def prepare(layer):
        def one(u, carry):
            live = len_ref[u] - cache * events
            mask = lax.broadcasted_iota(jnp.int32, (events, LANES), 0) < live
            left = pltpu.roll(raws[layer][u, :, 0:LANES].astype(F32), DH, 1)
            right = raws[layer][u, :, LANES : 2 * LANES].astype(F32)
            hists[layer][u, 0] = jnp.where(mask, left, 0.0).astype(BF16)
            hists[layer][u, 1] = jnp.where(mask, right, 0.0).astype(BF16)
            return carry

        lax.fori_loop(0, users, one, 0)

    def gather(layer):
        def one(k, carry):
            for d in range(nx):
                to_x = (x + d) % nx
                block = hists[layer][req_ref[((z + 2 * k) % nz) * nx + to_x]]
                if d == 0:
                    stay[layer, x, k] = block
                else:
                    stay_s[layer, d - 1, k] = block
                for j in range(2):
                    to_z = (z + side * (1 - 2 * j) + 2 * k + nz) % nz
                    pair_s[layer, d, j, k] = hists[layer][req_ref[to_z * nx + to_x], j]
            return carry

        lax.fori_loop(0, steps, one, 0)

    def kv_send(layer, own, g):
        span = pl.ds(g, 1)
        for d in range(nx):
            if own and d:
                remote(
                    stay_s.at[layer, d - 1, span], stay.at[layer, x, span],
                    stay_ss.at[layer], stay_rs.at[layer, g], at(0, d),
                ).start()
            for j in range(0 if own else 2):
                remote(
                    pair_s.at[layer, d, j, span], pair.at[layer, x, j, span],
                    pair_ss.at[layer], pair_rs.at[layer, g], at(side * (1 - 2 * j), d),
                ).start()

    def kv_point(point):
        for layer, own, batch in PACE[point]:
            for g in batch:
                if g < steps:
                    kv_send(layer, own, g)

    def kv_wait(layer, g):
        span = pl.ds(g, 1)
        drain(stay.at[layer, 0 : nx - 1, span], stay_rs.at[layer, g])
        drain(pair.at[layer, :, :, span], pair_rs.at[layer, g])

    loads[0].wait()
    prepare(0)
    gather(0)
    loads[1].wait()
    for p in range(PARTS):
        hid0[p, core, head] = own_tok[part_rows(p, core)]
    pl.semaphore_wait(barrier, len(peers))
    for p in range(PARTS):
        for d in range(1, nh):
            to = (head + d) % CORES
            remote(own_tok.at[part_rows(p, to)], hid0.at[p, to, head], tok_ss, tok_rs.at[p], h_peer(d)).start()
    loads[4].wait()
    wo0[head] = wo_own[0]
    for d in range(1, nh // CORES):
        remote(wo0.at[head], wo0.at[head], wo_sem.at[0], wo_sem.at[1], h_peer(CORES * d)).start()
    remote(wo0.at[head], wo0.at[head], wo_sem.at[0], wo_sem.at[2], sibling).start()
    kv_point(0)
    loads[2].wait()
    prepare(1)
    gather(1)
    loads[3].wait()
    for b in range(nh):
        wo1_s[b // CORES, b % CORES] = wo_own[1, :, b * LANES : (b + 1) * LANES]
    wo1[head] = wo1_s[chip]

    def project(layer, p, halves):
        hidden = jnp.concatenate([halves[p, :, b].reshape(rows, LANES) for b in range(nh)], axis=1)
        left = silu(dot(hidden, w_in[layer, :, 0:LANES]))
        right = pltpu.roll(silu(dot(hidden, w_in[layer, :, LANES : 2 * LANES])), DH, 1)
        low = lane_halves(rows)
        q = (jnp.where(low, right, left).astype(BF16).astype(F32) * (0.5 * DH**-0.5)).astype(BF16)
        gates = jnp.where(low, left, right).astype(BF16)
        q_all[layer, p, 0] = q
        for c in range(CORES):
            gate_s[layer, p, c] = gates[c * half : (c + 1) * half]
        for k in [k for k in FIRST if k < steps]:
            remote(
                q_all.at[layer, p, 0], q_all.at[layer, p, steps - k],
                q_ss.at[layer], q_rs.at[layer, p, steps - k], at(2 * k, 0),
            ).start()

    def send_gates(layer):
        for p in range(PARTS):
            gate_all[layer, p, head] = gate_s[layer, p, core]
            for d in range(1, nh):
                remote(
                    gate_s.at[layer, p, (head + d) % CORES], gate_all.at[layer, p, head],
                    g_ss.at[layer], g_rs.at[layer, p], h_peer(d),
                ).start()

    def attend(layer, k, q):
        low = lane_halves(q.shape[0])
        zero = jnp.zeros_like(q)
        outs = []
        for j, q_one in ((0, jnp.where(low, zero, q)), (1, jnp.where(low, q, zero))):
            kvs, weights = [], []
            for s in range(0, nx, 2):
                for keys in (stay[layer, s : s + 2, k, j], pair[layer, s : s + 2, j, k]):
                    kv = keys.reshape(2 * events, LANES)
                    t = dot(q_one, kv, ((1,), (1,)))
                    kvs.append(kv)
                    weights.append((t + t * jnp.tanh(t)).astype(BF16))
            outs.append(dot(jnp.concatenate(weights, axis=1), jnp.concatenate(kvs, axis=0)))
        block = jnp.where(low, outs[0], outs[1])
        centres = centre(block)
        return block - spread(centres), centres.astype(F32)

    def give(layer, k, p, block, centres):
        part_s[layer, p, k - 1, 0:rows] = block.astype(BF16)
        part_s[layer, p, k - 1, rows : rows + EXTRA] = jnp.concatenate(
            [centres, jnp.zeros_like(centres)], axis=0
        ).astype(BF16)
        remote(
            part_s.at[layer, p, k - 1], part_r.at[layer, p, k - 1], p_ss.at[layer], p_rs.at[layer, p], at(2 * k, 0)
        ).start()

    def both(layer, k):
        q = jnp.concatenate([q_all[layer, p, k] for p in range(PARTS)], axis=0)
        block, centres = attend(layer, k, q)
        return [(block[p * rows : (p + 1) * rows], centres[:, p * rows : (p + 1) * rows]) for p in range(PARTS)]

    def attention(layer):
        def own():
            kv_wait(layer, 0)
            for p, (block, centres) in enumerate(both(layer, 0)):
                acc[p] = block
                mid[p] = centres

        waited = [0]
        for k, p in ORDER[layer]:
            if k == 0:
                if layer == 0:
                    kv_point(2)
                own()
            elif k < steps:
                if k not in waited:
                    kv_wait(layer, k)
                    waited.append(k)
                for e in range(PARTS) if p < 0 else (p,):
                    drain(q_all.at[layer, e, k], q_rs.at[layer, e, k])
                if p < 0:
                    for e, (block, centres) in enumerate(both(layer, k)):
                        give(layer, k, e, block, centres)
                else:
                    give(layer, k, p, *attend(layer, k, q_all[layer, p, k]))

    def send_attended(layer):
        for p in range(PARTS):
            block, centres = acc[p], mid[p]
            if steps > 1:
                drain(part_r.at[layer, p], p_rs.at[layer, p])
            for k in range(steps - 1):
                block = block + part_r[layer, p, k, 0:rows].astype(F32)
                centres = centres + part_r[layer, p, k, rows : rows + EXTRA].astype(F32)[0:8]
            high = centres.astype(BF16).astype(F32)
            pairs = jnp.concatenate([high, centres - high], axis=0)
            for c in range(CORES):
                att_s[layer, p, c, 0:half] = block[c * half : (c + 1) * half].astype(BF16)
                shifted = pairs if c == 0 else pltpu.roll(pairs, rows - c * half, 1)
                att_s[layer, p, c, half : half + EXTRA] = shifted.astype(BF16)
            for d in range(1, nh):
                remote(
                    att_s.at[layer, p, (head + d) % CORES], att_all.at[layer, p, head],
                    a_ss.at[layer], a_rs.at[layer, p], h_peer(d),
                ).start()
            att_all[layer, p, head] = att_s[layer, p, core]

    def normed(layer, p):
        total = jnp.zeros((half, LANES), F32)
        squares = jnp.zeros((half, LANES), F32)
        drain(gate_all.at[layer, p, 0 : nh - 1], g_rs.at[layer, p])
        drain(att_all.at[layer, p, 0 : nh - 1], a_rs.at[layer, p])
        for b in range(nh):
            block = att_all[layer, p, b, 0:half].astype(F32) + spread(
                att_all[layer, p, b, half : half + EXTRA][:, 0:half]
            )
            hid_f[b] = block
            total = total + block
            squares = squares + block * block
        width = nh * LANES
        mean = jnp.sum(total, axis=1, keepdims=True) * (1.0 / width)
        var = jnp.sum(squares, axis=1, keepdims=True) * (1.0 / width) - mean * mean
        scale = lax.rsqrt(var + 1e-05)
        return jnp.concatenate(
            [((hid_f[b] - mean) * scale * gate_all[layer, p, b].astype(F32)).astype(BF16) for b in range(nh)], axis=1
        )

    for p in range(PARTS):
        drain(hid0.at[p, 0, 0 : nh - 1], tok_rs.at[p])
        remote(hid0.at[p, core], hid0.at[p, core], fwd_ss, fwd_rs.at[p], sibling).start()
    for p in range(PARTS):
        drain(hid0.at[p, 0], fwd_rs.at[p])
        project(0, p, hid0)
    kv_point(1)
    send_gates(0)
    attention(0)
    if nh > CORES:
        drain(wo0.at[0 : nh // CORES - 1], wo_sem.at[1])
    for d in range(1, nh // CORES):
        src = (head + CORES * d) % nh
        remote(wo0.at[src], wo0.at[src], wo_sem.at[0], wo_sem.at[2], sibling).start()
    send_attended(0)
    kv_point(3)
    drain(wo0.at[0 : nh // CORES], wo_sem.at[2])
    for p in range(PARTS):
        gated = normed(0, p)
        full = wo0[...].reshape(nh * LANES, nh * LANES)
        for b in range(0, nh, 2):
            branch = dot(gated, full[:, b * LANES : (b + 2) * LANES])
            for e in range(2):
                hid[p, core, b + e] = (
                    hid0[p, core, b + e].astype(F32) + branch[:, e * LANES : (e + 1) * LANES]
                ).astype(BF16)
        remote(hid.at[p, core], hid.at[p, core], hid_ss, hid_rs.at[p], sibling).start()
    kv_point(4)
    for p in range(PARTS):
        drain(hid.at[p, 0], hid_rs.at[p])
        project(1, p, hid)
    kv_point(5)
    send_gates(1)
    for d in range(1, nh):
        remote(wo1_s.at[((head + d) % nh) // CORES], wo1.at[head], wt_sem.at[0], wt_sem.at[1], h_peer(d)).start()
    attention(1)
    send_attended(1)
    drain(wo1.at[0 : nh - 1], wt_sem.at[1])
    for p in range(PARTS):
        gated = normed(1, p)

        def final(c):
            branch = dot(gated, wo1[:, c].reshape(nh * LANES, LANES))
            return (hid[p, core, chip * CORES + c].astype(F32) + branch).astype(BF16)

        last_s[p] = final(1 - core)
        remote(last_s.at[p], last_r.at[p], last_sem.at[0], last_sem.at[1], sibling).start()
        out_ref[part_rows(p, core)] = final(core)

    drain(hid0.at[:, 0, 0 : nh - 1], tok_ss)
    drain(hid0.at[:, 0], fwd_ss)
    drain(wo0.at[0 : nh - 1], wo_sem.at[0])
    drain(wo1.at[0 : nh - 1], wt_sem.at[0])
    drain(hid.at[:, 0], hid_ss)
    for layer in range(LAYERS):
        drain(stay_s.at[layer], stay_ss.at[layer])
        drain(pair_s.at[layer], pair_ss.at[layer])
        if steps > 1:
            drain(q_all.at[layer, :, 0 : steps - 1], q_ss.at[layer])
            drain(part_s.at[layer], p_ss.at[layer])
        drain(gate_all.at[layer, :, 0 : nh - 1], g_ss.at[layer])
        drain(att_all.at[layer, :, 0 : nh - 1], a_ss.at[layer])
    drain(last_r, last_sem.at[1])
    drain(last_s, last_sem.at[0])
    for p in range(PARTS):
        out_ref[part_rows(p, 1 - core)] = last_r[p]


def body(x_size, nc, nh, tokens, request_user, hist_len, history, w_in, w_out):
    nx = x_size
    nz = nc // nx
    steps = nz // 2
    rows = tokens.shape[0] // PARTS
    half = rows // CORES
    users, events = history.shape[1], history.shape[2]
    width = nh * LANES
    hbm = pl.BlockSpec(memory_space=pltpu.HBM)
    smem = pl.BlockSpec(memory_space=pltpu.SMEM)
    sem = pltpu.SemaphoreType.DMA
    vmem = pltpu.VMEM
    return pl.pallas_call(
        functools.partial(kernel, (nz, nx, nh)),
        out_shape=jax.ShapeDtypeStruct((tokens.shape[0], LANES), BF16),
        in_specs=[smem, smem, hbm, hbm, hbm, hbm],
        out_specs=pl.BlockSpec(memory_space=pltpu.VMEM),
        scratch_shapes=[
            vmem((users, events, 2 * LANES), BF16),
            vmem((users, events, 2 * LANES), BF16),
            vmem((users, 2, events, LANES), BF16),
            vmem((users, 2, events, LANES), BF16),
            vmem((LAYERS, nx - 1, steps, 2, events, LANES), BF16),
            vmem((LAYERS, nx, steps, 2, events, LANES), BF16),
            vmem((LAYERS, nx, 2, steps, events, LANES), BF16),
            vmem((LAYERS, nx, 2, steps, events, LANES), BF16),
            vmem((PARTS * rows, LANES), BF16),
            vmem((PARTS, CORES, nh, half, LANES), BF16),
            vmem((PARTS, CORES, nh, half, LANES), BF16),
            vmem((nh, half, LANES), F32),
            vmem((LAYERS, width, 2 * LANES), BF16),
            vmem((nh, LANES, width), BF16),
            vmem((LAYERS, LANES, width), BF16),
            vmem((nh // CORES, CORES, LANES, LANES), BF16),
            vmem((nh, CORES, LANES, LANES), BF16),
            vmem((LAYERS, PARTS, steps, rows, LANES), BF16),
            vmem((LAYERS, PARTS, CORES, half, LANES), BF16),
            vmem((LAYERS, PARTS, nh, half, LANES), BF16),
            vmem((LAYERS, PARTS, max(steps - 1, 1), rows + EXTRA, LANES), BF16),
            vmem((LAYERS, PARTS, max(steps - 1, 1), rows + EXTRA, LANES), BF16),
            vmem((LAYERS, PARTS, CORES, half + EXTRA, LANES), BF16),
            vmem((LAYERS, PARTS, nh, half + EXTRA, LANES), BF16),
            vmem((PARTS, rows, LANES), F32),
            vmem((PARTS, 8, rows), F32),
            vmem((PARTS, half, LANES), BF16),
            vmem((PARTS, half, LANES), BF16),
            sem((5,)),
            sem, sem((PARTS,)), sem, sem((PARTS,)),
            sem((LAYERS,)), sem((LAYERS, steps)),
            sem((LAYERS,)), sem((LAYERS, steps)),
            sem((LAYERS,)), sem((LAYERS, PARTS, steps)),
            sem((LAYERS,)), sem((LAYERS, PARTS)),
            sem((LAYERS,)), sem((LAYERS, PARTS)),
            sem((LAYERS,)), sem((LAYERS, PARTS)),
            sem((3,)), sem((2,)),
            sem, sem((PARTS,)), sem((2,)),
        ],
        compiler_params=pltpu.CompilerParams(
            collective_id=0, has_side_effects=True, vmem_limit_bytes=60 * 1024 * 1024
        ),
    )(request_user.reshape(-1), hist_len, tokens, history, w_in, w_out)


def solution(mesh):
    in_specs = (
        P("cache", "head"),
        P(),
        P(),
        P(None, None, "cache", "head"),
        P(None, None, "head"),
        P(None, "head", None),
    )
    run = functools.partial(body, X_SIZE, mesh.shape["cache"], mesh.shape["head"])
    return jax.shard_map(run, mesh=mesh, in_specs=in_specs, out_specs=P("cache", "head"), check_vma=False)
```

time: 78.9 us -> 74.6 us (0.946)
  Pallas kernels: 77.3 us -> 72.7 us
    pallas_call x1, Pallas kernels: 77.3 us -> 72.7 us  [body(): pl.pallas_call(functools.partial(kernel, (nz, nx, nh)), out_shape=jax.Sha...]
where the time goes in v4:
time: 74.6 us; the launch traced here: 74.2 us
  Pallas kernels  72.7 us (97%)
  local copies, waits for them, and re-layouts  1.47 us (2%)
    pallas_call x1, Pallas kernels, body(): pl.pallas_call(functools.partial(kernel, (nz, nx, nh)), out_shape=jax.Sha...  72.7 us

profile of v4, /device:TPU:1, one launch (start us, length us, event | category | flops | bytes accessed | tf_op | source)
XLA Modules:
  0.0 74.2 jit_solution(17193403905099959840)
XLA Ops:
  0.0 72.7 %shard_map.64 = bf16[256,128]{1,0:T(8,128)(2,1)} custom-call(s32[32]{0:T(128)} %bitcast.1, s32[16]{0:T(128)} %len_ref.1, bf16[256,128]{1,0:T(8,128)(2,1)} %tok_hbm.1, bf16[2,16,128,256]{3,2,1,0:T(8,128)(2,1)} %hist_hbm.1, bf16[2,1024,256]{2,1,0:T(8,128)(2,1)} %w_in_hbm.1, bf16[2,128,1024]{2,1,0:T(8,128)(2,1)} %w_out_hbm.1), custom_call_target="tpu_custom_call" | custom-call | tf_op jit(solution)/shard_map/pallas_call | solution.py:394
  72.8 1.5 %copy.8 = bf16[256,128]{1,0:T(8,128)(2,1)} copy(bf16[256,128]{1,0:T(8,128)(2,1)} %shard_map.64) | data formatting | bytes 131072

commit v5 on v4

--- a/solution.py
+++ b/solution.py
@@ -14,12 +14,11 @@
 CORES = 2
 PARTS = 2
 FIRST = (2, 1, 3)
-ORDER = (((2, -1), (1, -1), (3, -1), (0, -1)), ((0, -1), (2, -1), (1, -1), (3, -1)))
+ORDER = (((2, -1), (1, -1), (3, -1), (0, -1)), ((2, -1), (0, -1), (1, -1), (3, -1)))
 EXTRA = 16
 OWN, NEAR = True, False
 PACE = (
-    ((0, OWN, (2, 1, 3, 0)), (0, NEAR, (2, 1, 3, 0))), (),
-    ((1, NEAR, (0, 2, 1, 3)), (1, OWN, (0, 2, 1, 3))), (), (), (),
+    ((0, OWN, (2, 1, 3, 0)), (0, NEAR, (2, 1, 3, 0))), ((1, OWN, (2, 0, 1, 3)),), ((1, NEAR, (2, 0, 1, 3)),), (), (), (),
 )
 MESH = pl.DeviceIdType.MESH
 F32 = jnp.float32
@@ -244,6 +243,13 @@
         q = jnp.concatenate([q_all[layer, p, k] for p in range(PARTS)], axis=0)
         block, centres = attend(layer, k, q)
         return [(block[p * rows : (p + 1) * rows], centres[:, p * rows : (p + 1) * rows]) for p in range(PARTS)]
+
+    def forward_w_out():
+        if nh > CORES:
+            drain(wo0.at[0 : nh // CORES - 1], wo_sem.at[1])
+        for d in range(1, nh // CORES):
+            src = (head + CORES * d) % nh
+            remote(wo0.at[src], wo0.at[src], wo_sem.at[0], wo_sem.at[2], sibling).start()
 
     def attention(layer):
         def own():
@@ -319,12 +325,8 @@
         project(0, p, hid0)
     kv_point(1)
     send_gates(0)
+    forward_w_out()
     attention(0)
-    if nh > CORES:
-        drain(wo0.at[0 : nh // CORES - 1], wo_sem.at[1])
-    for d in range(1, nh // CORES):
-        src = (head + CORES * d) % nh
-        remote(wo0.at[src], wo0.at[src], wo_sem.at[0], wo_sem.at[2], sibling).start()
     send_attended(0)
     kv_point(3)
     drain(wo0.at[0 : nh // CORES], wo_sem.at[2])

time: 74.6 us -> 74.3 us (level)
  no operation moved by 1% of the time
where the time goes in v5:
time: 74.3 us; the launch traced here: 74.2 us
  Pallas kernels  72.7 us (98%)
  local copies, waits for them, and re-layouts  1.47 us (2%)
    pallas_call x1, Pallas kernels, body(): pl.pallas_call(functools.partial(kernel, (nz, nx, nh)), out_shape=jax.Sha...  72.7 us

profile of v5, /device:TPU:1, one launch (start us, length us, event | category | flops | bytes accessed | tf_op | source)
XLA Modules:
  0.0 74.2 jit_solution(5651799706492871769)
XLA Ops:
  0.0 72.7 %shard_map.64 = bf16[256,128]{1,0:T(8,128)(2,1)} custom-call(s32[32]{0:T(128)} %bitcast.1, s32[16]{0:T(128)} %len_ref.1, bf16[256,128]{1,0:T(8,128)(2,1)} %tok_hbm.1, bf16[2,16,128,256]{3,2,1,0:T(8,128)(2,1)} %hist_hbm.1, bf16[2,1024,256]{2,1,0:T(8,128)(2,1)} %w_in_hbm.1, bf16[2,128,1024]{2,1,0:T(8,128)(2,1)} %w_out_hbm.1), custom_call_target="tpu_custom_call" | custom-call | tf_op jit(solution)/shard_map/pallas_call | solution.py:396
  72.7 1.5 %copy.8 = bf16[256,128]{1,0:T(8,128)(2,1)} copy(bf16[256,128]{1,0:T(8,128)(2,1)} %shard_map.64) | data formatting | bytes 131072

commit v6 on v5

--- a/solution.py
+++ b/solution.py
@@ -14,7 +14,9 @@
 CORES = 2
 PARTS = 2
 FIRST = (2, 1, 3)
-ORDER = (((2, -1), (1, -1), (3, -1), (0, -1)), ((2, -1), (0, -1), (1, -1), (3, -1)))
+ORDER = (
+    ((2, -1), (1, -1), (3, -1), (0, -1)), ((2, 0), (0, -1), (1, 0), (3, 0), (2, 1), (1, 1), (3, 1)),
+)
 EXTRA = 16
 OWN, NEAR = True, False
 PACE = (

time: 74.3 us -> 74.9 us (level)
  no operation moved by 1% of the time
where the time goes in v6:
time: 74.9 us; the launch traced here: 74.7 us
  Pallas kernels  73.2 us (98%)
  local copies, waits for them, and re-layouts  1.47 us (2%)
    pallas_call x1, Pallas kernels, body(): pl.pallas_call(functools.partial(kernel, (nz, nx, nh)), out_shape=jax.Sha...  73.2 us

profile of v6, /device:TPU:1, one launch (start us, length us, event | category | flops | bytes accessed | tf_op | source)
XLA Modules:
  0.0 74.7 jit_solution(12144818920786430124)
XLA Ops:
  0.0 73.2 %shard_map.64 = bf16[256,128]{1,0:T(8,128)(2,1)} custom-call(s32[32]{0:T(128)} %bitcast.1, s32[16]{0:T(128)} %len_ref.1, bf16[256,128]{1,0:T(8,128)(2,1)} %tok_hbm.1, bf16[2,16,128,256]{3,2,1,0:T(8,128)(2,1)} %hist_hbm.1, bf16[2,1024,256]{2,1,0:T(8,128)(2,1)} %w_in_hbm.1, bf16[2,128,1024]{2,1,0:T(8,128)(2,1)} %w_out_hbm.1), custom_call_target="tpu_custom_call" | custom-call | tf_op jit(solution)/shard_map/pallas_call | solution.py:398
  73.3 1.5 %copy.8 = bf16[256,128]{1,0:T(8,128)(2,1)} copy(bf16[256,128]{1,0:T(8,128)(2,1)} %shard_map.64) | data formatting | bytes 131072
